TPU v7x, 32 devices: a whole 2x2x4 slice. The times are simulated.
32 devices in a mesh: groups: 2 (over x), context: 16 (over z, y, core).
Axes of the slice: x: 2, y: 2, z: 4, core: 2. Of those that a mesh axis runs over, the one named last changes fastest.
Arguments:
- projected: bfloat16 [4096, 3072], P(('groups', 'context')), parts along dimension 0, may hold values from -6 to 6
- short_filter: bfloat16 [3, 3072], replicated, may hold values from -3.5 to 3.5
- filter_taps: float32 [2048, 64], P('context'), may hold values from -2 to 2
- bank: int32 [1024], replicated, may hold values from 0 to 63
- skip: float32 [1024], replicated, may hold values from -1 to 1
Outputs:
- gated_output: bfloat16 [4096, 1024], P(('groups', 'context')), parts along dimension 0
There are 2 independent parts, one for each index of `groups`. A program takes and returns all parts, laid end to end along the dimension named above; an argument that names none is the same for every part. Nothing has to cross between parts.
All inputs are finite; a program needn't handle non-finite values.
Results may differ from a plain program's by a relative error of at most 0.001.
Values may be sent and summed in bfloat16 or wider, within the bound.
A program may use at most 64 MiB of HBM per device.

v0:
```python
import math

import jax
import jax.numpy as jnp
from jax import lax
from jax.sharding import PartitionSpec as P

HIGHEST = lax.Precision.HIGHEST


def from_partner(array, axis, distance):
    return lax.ppermute(array, axis, [(i, i ^ 1 << distance) for i in range(lax.axis_size(axis))])


def from_behind(array, axis, by):
    count = lax.axis_size(axis)
    pairs = [(i, i + by) for i in range(count) if 0 <= i + by < count]
    return lax.ppermute(array, axis, pairs)


def phases(numer, period, sign):
    angle = sign * 2.0 * math.pi / period * (numer % period).astype(jnp.float32)
    return (jnp.cos(angle), jnp.sin(angle))


def local_table(length, sign):
    places = jnp.arange(length, dtype=jnp.int32)
    return phases(places[:, None] * places[None, :], length, sign)


def rotate(real, imag, cosine, sine):
    return (real * cosine - imag * sine, real * sine + imag * cosine)


def complex_product(left_real, left_imag, right_real, right_imag):
    out_real = jnp.dot(left_real, right_real, precision=HIGHEST) - jnp.dot(
        left_imag, right_imag, precision=HIGHEST
    )
    out_imag = jnp.dot(left_real, right_imag, precision=HIGHEST) + jnp.dot(
        left_imag, right_real, precision=HIGHEST
    )
    return (out_real, out_imag)


def forward_transform(real, imag, length_total, shards, my_index):
    levels = shards.bit_length() - 1
    steps = real.shape[0]
    for level in range(levels - 1, -1, -1):
        span = 1 << level
        other_real, other_imag = from_partner((real, imag), "context", level)
        upper = my_index >> level & 1 == 1
        cosine, sine = phases(my_index % span, 2 * span, -1.0)
        turned_real, turned_imag = rotate(other_real - real, other_imag - imag, cosine, sine)
        real = jnp.where(upper, turned_real, real + other_real)
        imag = jnp.where(upper, turned_imag, imag + other_imag)
    frequency = jnp.zeros((), jnp.int32)
    for level in range(levels):
        frequency = frequency | (my_index >> level & 1) << levels - 1 - level
    position = jnp.arange(steps, dtype=jnp.int32)
    cosine, sine = phases(position * frequency, length_total, -1.0)
    real, imag = rotate(real, imag, cosine[:, None], sine[:, None])
    table_cos, table_sin = local_table(steps, -1.0)
    real, imag = complex_product(table_cos, table_sin, real, imag)
    return (real, imag, frequency)


def inverse_transform(real, imag, frequency, length_total, shards, my_index):
    levels = shards.bit_length() - 1
    steps = real.shape[0]
    table_cos, table_sin = local_table(steps, 1.0)
    real, imag = complex_product(table_cos / steps, table_sin / steps, real, imag)
    position = jnp.arange(steps, dtype=jnp.int32)
    cosine, sine = phases(position * frequency, length_total, 1.0)
    real, imag = rotate(real, imag, cosine[:, None], sine[:, None])
    for level in range(levels):
        span = 1 << level
        other_real, other_imag = from_partner((real, imag), "context", level)
        upper = my_index >> level & 1 == 1
        cosine, sine = phases(my_index % span, 2 * span, 1.0)
        mine_real, mine_imag = rotate(real, imag, cosine, sine)
        theirs_real, theirs_imag = rotate(other_real, other_imag, cosine, sine)
        real_next = jnp.where(upper, 0.5 * (other_real - mine_real), 0.5 * (real + theirs_real))
        imag_next = jnp.where(upper, 0.5 * (other_imag - mine_imag), 0.5 * (imag + theirs_imag))
        real, imag = (real_next, imag_next)
    return (real, imag)


def per_device(projected, short_filter, filter_taps, bank, skip):
    steps = projected.shape[0]
    shards = lax.axis_size("context")
    my_index = lax.axis_index("context")
    length_total = steps * shards
    channels = skip.shape[0]
    banks = filter_taps.shape[1]
    earlier = from_behind(projected[steps - 2 :], "context", 1)
    joined = jnp.concatenate([earlier, projected], axis=0)
    weights = short_filter.astype(jnp.float32)
    featured = weights[0] * joined[2:] + weights[1] * joined[1:-1] + weights[2] * joined[:-2]
    query = featured[:, :channels]
    key_part = featured[:, channels : 2 * channels]
    value_part = featured[:, 2 * channels :]
    mixed = key_part * value_part
    signal = jnp.concatenate([mixed, filter_taps], axis=1)
    position = my_index * steps + jnp.arange(steps, dtype=jnp.int32)
    cosine, sine = phases(position, 2 * length_total, -1.0)
    real = jnp.concatenate([signal, signal * cosine[:, None]], axis=1)
    imag = jnp.concatenate([jnp.zeros_like(signal), signal * sine[:, None]], axis=1)
    spec_real, spec_imag, frequency = forward_transform(real, imag, length_total, shards, my_index)
    width = channels + banks
    selector = (bank[None, :] == jnp.arange(banks, dtype=jnp.int32)[:, None]).astype(jnp.float32)
    real_parts = []
    imag_parts = []
    for branch in range(2):
        offset = branch * width
        data_real = spec_real[:, offset : offset + channels]
        data_imag = spec_imag[:, offset : offset + channels]
        filter_real = jnp.dot(
            spec_real[:, offset + channels : offset + width], selector, precision=HIGHEST
        )
        filter_imag = jnp.dot(
            spec_imag[:, offset + channels : offset + width], selector, precision=HIGHEST
        )
        real_parts.append(data_real * filter_real - data_imag * filter_imag)
        imag_parts.append(data_real * filter_imag + data_imag * filter_real)
    product_real = jnp.concatenate(real_parts, axis=1)
    product_imag = jnp.concatenate(imag_parts, axis=1)
    back_real, back_imag = inverse_transform(
        product_real, product_imag, frequency, length_total, shards, my_index
    )
    cos_back, sin_back = phases(position, 2 * length_total, 1.0)
    second = (
        back_real[:, channels:] * cos_back[:, None] - back_imag[:, channels:] * sin_back[:, None]
    )
    convolved = 0.5 * (back_real[:, :channels] + second)
    return (query * (convolved + skip * mixed)).astype(jnp.bfloat16)


def solution(mesh):
    in_specs = (P(("groups", "context"), None), P(), P("context", None), P(), P())
    out_specs = P(("groups", "context"), None)
    return jax.shard_map(
        per_device, mesh=mesh, in_specs=in_specs, out_specs=out_specs, check_vma=False
    )
```

profile of v0, /device:TPU:0, one launch (start us, length us, event | category | flops | bytes accessed | tf_op | source)
XLA Modules:
  0.0 447.7 jit_solution(2920846924977963047)
XLA Ops:
  0.0 0.8 slice.62
  0.8 2.4 collective-permute-start
  3.2 0.9 fusion.102
  4.1 0.1 multiply_sine_fusion.6
  4.1 0.9 copy.7
  5.0 2.3 multiply_add_fusion
  7.3 0.1 slice_multiply_fusion.3
  7.4 0.1 fusion.18
  7.5 1.3 concatenate.21
  8.8 5.8 %collective-permute-start.1 = (f32[128,2176]{1,0:T(8,128)}, f32[128,2176]{1,0:T(8,128)}, u32[]{:S(2)}, u32[]{:S(2)}) collective-permute-start(f32[128,2176]{1,0:T(8,128)} %concatenate.21), channel_id=1, source_target_pairs={{0,8},{1,9},{2,10},{3,11},{4,12},{5,13},{6,14},{7,15},{8,0},{9,1},... | collective-permute-start | bytes 3342344 | tf_op jit(solution)/shard_map/ppermute | solution.py:12
  14.5 1.2 concatenate.22
  16.0 72.0 %collective-permute-done.1 = f32[128,2176]{1,0:T(8,128)} collective-permute-done((f32[128,2176]{1,0:T(8,128)}, f32[128,2176]{1,0:T(8,128)}, u32[]{:S(2)}, u32[]{:S(2)}) %collective-permute-start.1) | collective-permute-done | bytes 1114144 | tf_op jit(solution)/shard_map/ppermute | solution.py:12
  88.0 22.7 %collective-permute-done.2 = f32[128,2176]{1,0:T(8,128)} collective-permute-done((f32[128,2176]{1,0:T(8,128)}, f32[128,2176]{1,0:T(8,128)}, u32[]{:S(2)}, u32[]{:S(2)}) %collective-permute-start.2) | collective-permute-done | bytes 1114144 | tf_op jit(solution)/shard_map/ppermute | solution.py:12
  110.7 3.4 add_select_fusion.7
  114.2 0.7 collective-permute-start.3
  114.8 1.4 collective-permute-start.4
  116.4 25.5 %collective-permute-done.3 = f32[128,2176]{1,0:T(8,128)S(1)} collective-permute-done((f32[128,2176]{1,0:T(8,128)}, f32[128,2176]{1,0:T(8,128)S(1)}, u32[]{:S(2)}, u32[]{:S(2)}) %collective-permute-start.3) | collective-permute-done | bytes 1114144 | tf_op jit(solution)/shard_map/ppermute | solution.py:12
  141.9 1.0 copy-done.1
  142.9 20.9 %collective-permute-done.4 = f32[128,2176]{1,0:T(8,128)} collective-permute-done((f32[128,2176]{1,0:T(8,128)}, f32[128,2176]{1,0:T(8,128)}, u32[]{:S(2)}, u32[]{:S(2)}) %collective-permute-start.4) | collective-permute-done | bytes 1114144 | tf_op jit(solution)/shard_map/ppermute | solution.py:12
  163.8 3.7 add_select_fusion.5
  167.5 2.1 collective-permute-start.5
  169.8 25.4 %collective-permute-done.5 = f32[128,2176]{1,0:T(8,128)} collective-permute-done((f32[128,2176]{1,0:T(8,128)S(1)}, f32[128,2176]{1,0:T(8,128)}, u32[]{:S(2)}, u32[]{:S(2)}) %collective-permute-start.5) | collective-permute-done | bytes 1114144 | tf_op jit(solution)/shard_map/ppermute | solution.py:12
  195.2 21.8 %collective-permute-done.6 = f32[128,2176]{1,0:T(8,128)} collective-permute-done((f32[128,2176]{1,0:T(8,128)}, f32[128,2176]{1,0:T(8,128)}, u32[]{:S(2)}, u32[]{:S(2)}) %collective-permute-start.6) | collective-permute-done | bytes 1114144 | tf_op jit(solution)/shard_map/ppermute | solution.py:12
  217.0 3.7 add_select_fusion.3
  220.7 0.5 collective-permute-start.8
  221.2 0.1 multiply_sine_fusion.5
  221.3 0.1 multiply_sine_fusion.4
  221.3 3.6 collective-permute-done.7
  224.9 0.5 collective-permute-done.8
  225.4 2.3 add_select_fusion.1
  227.7 1.4 fusion.36
  229.1 1.4 fusion.37
  230.5 1.4 convolution_subtract_fusion
  232.0 0.4 fusion.20
  232.4 0.4 fusion.22
  232.8 1.4 convolution_add_fusion
  234.2 0.4 fusion.19
  234.7 0.6 multiply_subtract_fusion.3
  235.2 1.3 fusion
  236.5 1.5 fusion.1
  238.0 1.3 convolution_subtract_fusion.1
  239.3 1.6 multiply_add_fusion.2
  240.9 0.2 collective-permute-start.10
  241.1 0.4 collective-permute-start.9
  241.5 2.1 collective-permute-done.10
  243.6 1.5 collective-permute-done.9
  245.1 1.6 multiply_select_fusion.5
  246.7 1.8 collective-permute-start.11
  248.5 0.3 collective-permute-start.12
  248.9 24.1 %collective-permute-done.11 = f32[128,2048]{1,0:T(8,128)} collective-permute-done((f32[128,2048]{1,0:T(8,128)}, f32[128,2048]{1,0:T(8,128)}, u32[]{:S(2)}, u32[]{:S(2)}) %collective-permute-start.11) | collective-permute-done | bytes 1048608 | tf_op jit(solution)/shard_map/ppermute | solution.py:12
  273.0 21.7 %collective-permute-done.12 = f32[128,2048]{1,0:T(8,128)} collective-permute-done((f32[128,2048]{1,0:T(8,128)S(1)}, f32[128,2048]{1,0:T(8,128)}, u32[]{:S(2)}, u32[]{:S(2)}) %collective-permute-start.12) | collective-permute-done | bytes 1048608 | tf_op jit(solution)/shard_map/ppermute | solution.py:12
  294.7 3.9 multiply_select_fusion.3
  298.7 1.8 collective-permute-start.13
  300.5 0.2 collective-permute-start.14
  300.8 24.1 %collective-permute-done.13 = f32[128,2048]{1,0:T(8,128)S(1)} collective-permute-done((f32[128,2048]{1,0:T(8,128)}, f32[128,2048]{1,0:T(8,128)S(1)}, u32[]{:S(2)}, u32[]{:S(2)}) %collective-permute-start.13) | collective-permute-done | bytes 1048608 | tf_op jit(solution)/shard_map/ppermute | solution.py:12
  325.0 1.0 copy-done.2
  326.0 19.9 %collective-permute-done.14 = f32[128,2048]{1,0:T(8,128)} collective-permute-done((f32[128,2048]{1,0:T(8,128)}, f32[128,2048]{1,0:T(8,128)}, u32[]{:S(2)}, u32[]{:S(2)}) %collective-permute-start.14) | collective-permute-done | bytes 1048608 | tf_op jit(solution)/shard_map/ppermute | solution.py:12
  345.9 3.9 multiply_select_fusion.1
  349.8 3.7 collective-permute-start.15
  353.7 0.1 multiply_sine_fusion.3
  353.8 67.8 %collective-permute-done.15 = f32[128,2048]{1,0:T(8,128)} collective-permute-done((f32[128,2048]{1,0:T(8,128)}, f32[128,2048]{1,0:T(8,128)}, u32[]{:S(2)}, u32[]{:S(2)}) %collective-permute-start.15) | collective-permute-done | bytes 1048608 | tf_op jit(solution)/shard_map/ppermute | solution.py:12
  421.5 21.4 %collective-permute-done.16 = f32[128,2048]{1,0:T(8,128)} collective-permute-done((f32[128,2048]{1,0:T(8,128)S(1)}, f32[128,2048]{1,0:T(8,128)}, u32[]{:S(2)}, u32[]{:S(2)}) %collective-permute-start.16) | collective-permute-done | bytes 1048608 | tf_op jit(solution)/shard_map/ppermute | solution.py:12
  443.0 2.3 multiply_select_fusion
  445.2 2.5 fusion.13
  (13 shorter events, 0.1 us)
Async XLA Ops:
  0.8 4.2 collective-permute-start
  8.8 102.0 %copy-start = (f32[128,2176]{1,0:T(8,128)S(1)}, f32[128,2176]{1,0:T(8,128)}, u32[]{:S(2)}) copy-start(f32[128,2176]{1,0:T(8,128)} %concatenate.21) | copy-start | bytes 3342340
  8.8 79.2 %collective-permute-start.1 = (f32[128,2176]{1,0:T(8,128)}, f32[128,2176]{1,0:T(8,128)}, u32[]{:S(2)}, u32[]{:S(2)}) collective-permute-start(f32[128,2176]{1,0:T(8,128)} %concatenate.21), channel_id=1, source_target_pairs={{0,8},{1,9},{2,10},{3,11},{4,12},{5,13},{6,14},{7,15},{8,0},{9,1},... | collective-permute-start | bytes 3342344 | tf_op jit(solution)/shard_map/ppermute | solution.py:12
  15.8 94.9 %collective-permute-start.2 = (f32[128,2176]{1,0:T(8,128)}, f32[128,2176]{1,0:T(8,128)}, u32[]{:S(2)}, u32[]{:S(2)}) collective-permute-start(f32[128,2176]{1,0:T(8,128)} %concatenate.22), channel_id=1, source_target_pairs={{0,8},{1,9},{2,10},{3,11},{4,12},{5,13},{6,14},{7,15},{8,0},{9,1},... | collective-permute-start | bytes 3342344 | tf_op jit(solution)/shard_map/ppermute | solution.py:12
  114.2 27.7 %collective-permute-start.3 = (f32[128,2176]{1,0:T(8,128)}, f32[128,2176]{1,0:T(8,128)S(1)}, u32[]{:S(2)}, u32[]{:S(2)}) collective-permute-start(f32[128,2176]{1,0:T(8,128)} %get-tuple-element.17), channel_id=1, source_target_pairs={{0,4},{1,5},{2,6},{3,7},{4,0},{5,1},{6,2},{7,3},{8,12},{9,13},{10,... | collective-permute-start | bytes 3342344 | tf_op jit(solution)/shard_map/ppermute | solution.py:12
  114.8 49.0 %collective-permute-start.4 = (f32[128,2176]{1,0:T(8,128)}, f32[128,2176]{1,0:T(8,128)}, u32[]{:S(2)}, u32[]{:S(2)}) collective-permute-start(f32[128,2176]{1,0:T(8,128)} %get-tuple-element.18), channel_id=1, source_target_pairs={{0,4},{1,5},{2,6},{3,7},{4,0},{5,1},{6,2},{7,3},{8,12},{9,13},{10,... | collective-permute-start | bytes 3342344 | tf_op jit(solution)/shard_map/ppermute | solution.py:12
  141.9 1.0 copy-start.1
  167.5 27.7 %collective-permute-start.5 = (f32[128,2176]{1,0:T(8,128)S(1)}, f32[128,2176]{1,0:T(8,128)}, u32[]{:S(2)}, u32[]{:S(2)}) collective-permute-start(f32[128,2176]{1,0:T(8,128)S(1)} %get-tuple-element.9), channel_id=1, source_target_pairs={{0,2},{1,3},{2,0},{3,1},{4,6},{5,7},{6,4},{7,5},{8,10},{9,11},{10,... | collective-permute-start | bytes 3342344 | tf_op jit(solution)/shard_map/ppermute | solution.py:12
  169.6 47.4 %collective-permute-start.6 = (f32[128,2176]{1,0:T(8,128)}, f32[128,2176]{1,0:T(8,128)}, u32[]{:S(2)}, u32[]{:S(2)}) collective-permute-start(f32[128,2176]{1,0:T(8,128)} %get-tuple-element.10), channel_id=1, source_target_pairs={{0,2},{1,3},{2,0},{3,1},{4,6},{5,7},{6,4},{7,5},{8,10},{9,11},{10,... | collective-permute-start | bytes 3342344 | tf_op jit(solution)/shard_map/ppermute | solution.py:12
  220.7 4.2 collective-permute-start.7
  220.7 4.7 %collective-permute-start.8 = (f32[128,2176]{1,0:T(8,128)}, f32[128,2176]{1,0:T(8,128)}, u32[]{:S(2)}, u32[]{:S(2)}) collective-permute-start(f32[128,2176]{1,0:T(8,128)} %get-tuple-element.8), channel_id=1, source_target_pairs={{0,1},{1,0},{2,3},{3,2},{4,5},{5,4},{6,7},{7,6},{8,9},{9,8},{10,11... | collective-permute-start | bytes 3342344 | tf_op jit(solution)/shard_map/ppermute | solution.py:12
  230.5 1.5 copy-start.3
  240.9 2.7 collective-permute-start.10
  241.1 4.0 collective-permute-start.9
  246.7 26.3 %collective-permute-start.11 = (f32[128,2048]{1,0:T(8,128)}, f32[128,2048]{1,0:T(8,128)}, u32[]{:S(2)}, u32[]{:S(2)}) collective-permute-start(f32[128,2048]{1,0:T(8,128)} %get-tuple-element.16), channel_id=1, source_target_pairs={{0,2},{1,3},{2,0},{3,1},{4,6},{5,7},{6,4},{7,5},{8,10},{9,11},{10,... | collective-permute-start | bytes 3145736 | tf_op jit(solution)/shard_map/ppermute | solution.py:12
  248.5 46.2 %collective-permute-start.12 = (f32[128,2048]{1,0:T(8,128)S(1)}, f32[128,2048]{1,0:T(8,128)}, u32[]{:S(2)}, u32[]{:S(2)}) collective-permute-start(f32[128,2048]{1,0:T(8,128)S(1)} %get-tuple-element.15), channel_id=1, source_target_pairs={{0,2},{1,3},{2,0},{3,1},{4,6},{5,7},{6,4},{7,5},{8,10},{9,11},{10,... | collective-permute-start | bytes 3145736 | tf_op jit(solution)/shard_map/ppermute | solution.py:12
  298.7 26.3 %collective-permute-start.13 = (f32[128,2048]{1,0:T(8,128)}, f32[128,2048]{1,0:T(8,128)S(1)}, u32[]{:S(2)}, u32[]{:S(2)}) collective-permute-start(f32[128,2048]{1,0:T(8,128)} %get-tuple-element.14), channel_id=1, source_target_pairs={{0,4},{1,5},{2,6},{3,7},{4,0},{5,1},{6,2},{7,3},{8,12},{9,13},{10,... | collective-permute-start | bytes 3145736 | tf_op jit(solution)/shard_map/ppermute | solution.py:12
  300.5 45.4 %collective-permute-start.14 = (f32[128,2048]{1,0:T(8,128)}, f32[128,2048]{1,0:T(8,128)}, u32[]{:S(2)}, u32[]{:S(2)}) collective-permute-start(f32[128,2048]{1,0:T(8,128)} %get-tuple-element.13), channel_id=1, source_target_pairs={{0,4},{1,5},{2,6},{3,7},{4,0},{5,1},{6,2},{7,3},{8,12},{9,13},{10,... | collective-permute-start | bytes 3145736 | tf_op jit(solution)/shard_map/ppermute | solution.py:12
  325.0 1.0 copy-start.2
  349.8 71.8 %collective-permute-start.15 = (f32[128,2048]{1,0:T(8,128)}, f32[128,2048]{1,0:T(8,128)}, u32[]{:S(2)}, u32[]{:S(2)}) collective-permute-start(f32[128,2048]{1,0:T(8,128)} %get-tuple-element.12), channel_id=1, source_target_pairs={{0,8},{1,9},{2,10},{3,11},{4,12},{5,13},{6,14},{7,15},{8,0},{9,1},... | collective-permute-start | bytes 3145736 | tf_op jit(solution)/shard_map/ppermute | solution.py:12
  353.5 89.4 %collective-permute-start.16 = (f32[128,2048]{1,0:T(8,128)S(1)}, f32[128,2048]{1,0:T(8,128)}, u32[]{:S(2)}, u32[]{:S(2)}) collective-permute-start(f32[128,2048]{1,0:T(8,128)S(1)} %get-tuple-element.11), channel_id=1, source_target_pairs={{0,8},{1,9},{2,10},{3,11},{4,12},{5,13},{6,14},{7,15},{8,0},{9,1},... | collective-permute-start | bytes 3145736 | tf_op jit(solution)/shard_map/ppermute | solution.py:12
  353.8 91.5 %copy-start.4 = (f32[1024]{0:T(1024)S(1)}, f32[1024]{0:T(1024)}, u32[]{:S(2)}) copy-start(f32[1024]{0:T(1024)} %param.9) | copy-start | bytes 12292
where the time goes:
time: 448 us
  waiting for transfers between devices  375 us (84%)
  other arithmetic  30 us (7%)
  starting transfers between devices  21.2 us (5%)
  matrix products  13.1 us (3%)
  local copies, waits for them, and re-layouts  7.09 us (2%)
    ppermute x16, waiting for transfers between devices, from_partner(): lax.ppermute(array, axis, [(i, i ^ 1 << distance) for i in range(lax.axis...  375 us
    ppermute x16, starting transfers between devices, from_partner(): lax.ppermute(array, axis, [(i, i ^ 1 << distance) for i in range(lax.axis...  18.9 us
    select_n x4, other arithmetic, forward_transform(): real = jnp.where(upper, turned_real, real + other_real)  13.1 us
    select_n x3, other arithmetic, inverse_transform(): jnp.where(upper, 0.5 * (other_imag - mine_imag), 0.5 * (imag + theirs_imag))  9.45 us
  transfers between devices with their start and end apart: 17, of which 16 were waited for; matrix products, arithmetic and copies ran while one was open for 1% of the time, Pallas kernels for 0%

commit v1 on v0

--- a/solution.py
+++ b/solution.py
@@ -1,8 +1,13 @@
+import functools
 import math
 
 import jax
 import jax.numpy as jnp
+import ml_dtypes
+import numpy as np
 from jax import lax
+from jax.experimental import pallas as pl
+from jax.experimental.pallas import tpu as pltpu
 from jax.sharding import PartitionSpec as P
 
 HIGHEST = lax.Precision.HIGHEST
@@ -85,7 +90,7 @@
     return (real, imag)
 
 
-def per_device(projected, short_filter, filter_taps, bank, skip):
+def per_device_spectral(projected, short_filter, filter_taps, bank, skip):
     steps = projected.shape[0]
     shards = lax.axis_size("context")
     my_index = lax.axis_index("context")
@@ -135,6 +140,389 @@
     return (query * (convolved + skip * mixed)).astype(jnp.bfloat16)
 
 
+LANES = 128
+F32 = jnp.float32
+BF16 = jnp.bfloat16
+
+
+def split_rows(table):
+    high = table.astype(ml_dtypes.bfloat16)
+    low = (table - high.astype(np.float64)).astype(ml_dtypes.bfloat16)
+    return np.concatenate([high, high, low], axis=1)
+
+
+def block_tables(steps):
+    angle = np.pi / steps * (np.arange(steps)[:, None] + 0.5) * np.arange(steps)[None, :]
+    forward = np.concatenate([np.cos(angle), -np.sin(angle)], axis=0)
+    inverse = np.concatenate([np.cos(angle.T), -np.sin(angle.T)], axis=1) / steps
+    return split_rows(forward), split_rows(inverse)
+
+
+def stacked(values):
+    high = values.astype(BF16)
+    low = (values - high.astype(F32)).astype(BF16)
+    return jnp.concatenate([high, low, high], axis=0)
+
+
+def kernel(
+    shards,
+    projected,
+    short_filter,
+    taps,
+    bank,
+    skip,
+    forward,
+    inverse,
+    out,
+    halo,
+    signal_out,
+    signal_in,
+    taps_in,
+    query,
+    direct,
+    signal_spec,
+    taps_spec,
+    pairs,
+    result_out,
+    result_in,
+    halo_sem,
+    signal_sent,
+    signal_got,
+    taps_sent,
+    taps_passed,
+    taps_got,
+    result_sent,
+    result_got,
+):
+    me = lax.axis_index("context")
+    steps = projected.shape[0]
+    half = steps // 2
+    channels = out.shape[1]
+    chips = shards // 2
+    chip = lax.div(me, 2)
+    core = lax.rem(me, 2)
+    sibling = me + 1 - 2 * core
+    left_lanes = lax.broadcasted_iota(jnp.int32, (half, LANES), 1) < LANES // 2
+
+    def remote(src, dst, sent, got, target):
+        return pltpu.make_async_remote_copy(
+            src_ref=src,
+            dst_ref=dst,
+            send_sem=sent,
+            recv_sem=got,
+            device_id={"context": target},
+            device_id_type=pl.DeviceIdType.MESH,
+        )
+
+    def arrived(ref, got):
+        pltpu.make_async_copy(ref, ref, got).wait()
+
+    def turned(values):
+        return pltpu.roll(values, LANES // 2, 1)
+
+    def exchange(first, second):
+        return (
+            jnp.where(left_lanes, first, turned(second)),
+            jnp.where(left_lanes, turned(first), second),
+        )
+
+    barrier = pltpu.get_barrier_semaphore()
+    for off in range(1, shards):
+        pl.semaphore_signal(
+            barrier,
+            inc=1,
+            device_id={"context": lax.rem(me + off, shards)},
+            device_id_type=pl.DeviceIdType.MESH,
+        )
+    values = jnp.concatenate([taps[:half, :], taps[half:, :]], axis=1)
+    high = values.astype(BF16)
+    taps_in[me] = jnp.concatenate([high, (values - high.astype(F32)).astype(BF16)], axis=0)
+    pl.semaphore_wait(barrier, shards - 1)
+
+    behind = remote(
+        projected.at[pl.ds(steps - 16, 16)],
+        halo,
+        halo_sem.at[0],
+        halo_sem.at[1],
+        lax.rem(me + 1, shards),
+    )
+    behind.start()
+
+    def taps_copy(off):
+        target = lax.rem(me + 2 * off, shards)
+        return remote(taps_in.at[me], taps_in.at[me], taps_sent.at[off], taps_got.at[me], target)
+
+    def taps_pass(off):
+        slot = lax.rem(me + shards - 2 * off, shards)
+        return remote(
+            taps_in.at[slot], taps_in.at[slot], taps_passed.at[off], taps_got.at[slot], sibling
+        )
+
+    taps_pass(0).start()
+
+    @pl.loop(1, chips)
+    def _(off):
+        taps_copy(off).start()
+
+    behind.wait()
+    row = lax.broadcasted_iota(jnp.int32, (steps, LANES), 0)
+
+    def featured(start):
+        columns = pl.ds(pl.multiple_of(start, LANES), LANES)
+        values = projected[:, columns].astype(F32)
+        earlier = halo[:, columns].astype(F32)
+        earlier = jnp.where(me == 0, 0.0, earlier)
+        weights = short_filter[:, columns].astype(F32)
+        last = earlier[15:16]
+        once = jnp.where(row == 0, last, pltpu.roll(values, 1, 0))
+        twice = jnp.where(
+            row == 0, earlier[14:15], jnp.where(row == 1, last, pltpu.roll(values, 2, 0))
+        )
+        return weights[0:1] * values + weights[1:2] * once + weights[2:3] * twice
+
+    def signal_copy(target, index):
+        return remote(
+            signal_out.at[target],
+            signal_in.at[me],
+            signal_sent.at[index],
+            signal_got.at[me],
+            target,
+        )
+
+    def make_signal(tile):
+        start = tile * LANES
+        mixed = featured(channels + start) * featured(2 * channels + start)
+        columns = pl.ds(pl.multiple_of(start, LANES), LANES)
+        direct[:, columns] = skip[pl.ds(tile, 1), :] * mixed
+        even, odd = exchange(mixed[:half], mixed[half:])
+        signal_out[2 * tile] = even
+        signal_out[2 * tile + 1] = odd
+
+    @pl.loop(1, chips)
+    def _(off):
+        tile = lax.rem(chip + off, chips)
+        make_signal(tile)
+        signal_copy(2 * tile, 2 * off).start()
+        signal_copy(2 * tile + 1, 2 * off + 1).start()
+
+    make_signal(chip)
+    signal_copy(sibling, 0).start()
+    own = pltpu.make_async_copy(signal_out.at[me], signal_in.at[me], signal_got.at[me])
+    own.start()
+
+    @pl.loop(0, chips)
+    def _(tile):
+        start = tile * LANES
+        query[:, pl.ds(pl.multiple_of(start, LANES), LANES)] = featured(start)
+
+    @pl.loop(1, chips)
+    def _(off):
+        slot = lax.rem(me + shards - 2 * off, shards)
+        arrived(taps_in.at[slot], taps_got.at[slot])
+        taps_pass(off).start()
+
+    banks = taps.shape[1]
+    own_bank = bank[pl.ds(chip, 1), :]
+    lane = lax.broadcasted_iota(jnp.int32, (1, LANES), 1)
+    in_half = (lane < LANES // 2).astype(jnp.int32)
+    own_bank = jnp.where(in_half + core == 1, own_bank, turned(own_bank))
+    own_bank = jnp.broadcast_to(own_bank, (banks, LANES))
+    pick = (lax.broadcasted_iota(jnp.int32, (banks, LANES), 0) == own_bank).astype(F32)
+    nothing = jnp.zeros_like(pick)
+    pick = jnp.concatenate(
+        [
+            jnp.concatenate([pick, nothing], axis=1),
+            jnp.concatenate([nothing, pick], axis=1),
+        ],
+        axis=0,
+    ).astype(BF16)
+
+    def taps_block(slot):
+        chosen = jnp.dot(taps_in[slot], pick, preferred_element_type=F32).astype(BF16)
+        high = [chosen[:half, :LANES], chosen[:half, LANES:]]
+        low = [chosen[half:, :LANES], chosen[half:, LANES:]]
+        return jnp.concatenate(high + low + high, axis=0)
+
+    def transform(low_slot, block, spec):
+        both = jnp.concatenate([block(low_slot), block(low_slot + 1)], axis=1)
+        both = jnp.dot(forward[...], both, preferred_element_type=F32)
+        spec[low_slot] = both[:, :LANES]
+        spec[low_slot + 1] = both[:, LANES:]
+
+    @pl.loop(0, chips)
+    def _(off):
+        source = lax.rem(chip + chips - off, chips)
+        slot = 2 * source + 1 - core
+        arrived(taps_in.at[slot], taps_got.at[slot])
+        transform(2 * source, taps_block, taps_spec)
+
+    sign = lax.broadcasted_iota(jnp.int32, (steps, LANES), 0)
+    sign = (1 - 2 * lax.rem(sign, 2)).astype(F32)
+    left = lax.broadcasted_iota(jnp.int32, (steps, LANES), 1) < LANES // 2
+    zero = jnp.zeros((steps, LANES), F32)
+
+    def window(slot, before):
+        real, imag = taps_spec[slot, :steps], taps_spec[slot, steps:]
+        if before is None:
+            return real, imag
+        return (
+            real - sign * taps_spec[before, steps:],
+            imag + sign * taps_spec[before, :steps],
+        )
+
+    real, imag = window(0, None)
+    pairs[0, :steps] = jnp.where(left, zero, real)
+    pairs[0, steps:] = jnp.where(left, zero, imag)
+    next_real, next_imag = window(1, 0)
+    pairs[1, :steps] = jnp.where(left, real, next_real)
+    pairs[1, steps:] = jnp.where(left, imag, next_imag)
+
+    @pl.loop(2, shards)
+    def _(slot):
+        real, imag = window(slot - 1, slot - 2)
+        next_real, next_imag = window(slot, slot - 1)
+        pairs[slot, :steps] = jnp.where(left, real, next_real)
+        pairs[slot, steps:] = jnp.where(left, imag, next_imag)
+
+    def signal_block(slot):
+        packed = signal_in[slot]
+        other = turned(packed)
+        return stacked(
+            jnp.concatenate(
+                [jnp.where(left_lanes, packed, other), jnp.where(left_lanes, other, packed)],
+                axis=0,
+            )
+        )
+
+    @pl.loop(0, chips)
+    def _(step):
+        off = lax.rem(step + 1, chips)
+        low_slot = 2 * lax.rem(chip + chips - off, chips)
+        arrived(signal_in.at[low_slot], signal_got.at[low_slot])
+        arrived(signal_in.at[low_slot + 1], signal_got.at[low_slot + 1])
+        transform(low_slot, signal_block, signal_spec)
+
+    def result_copy(target, index):
+        return remote(
+            result_out.at[target],
+            result_in.at[me],
+            result_sent.at[index],
+            result_got.at[me],
+            target,
+        )
+
+    def make_result(pair):
+        def add(slot, sums):
+            real, imag = sums
+            other = 2 * pair + 1 - slot
+            left_real, left_imag = signal_spec[slot, :steps], signal_spec[slot, steps:]
+            right_real, right_imag = pairs[other, :steps], pairs[other, steps:]
+            return (
+                real + (left_real * right_real - left_imag * right_imag),
+                imag + (left_real * right_imag + left_imag * right_real),
+            )
+
+        real, imag = lax.fori_loop(0, 2 * pair + 2, add, (zero, zero))
+        product = stacked(jnp.concatenate([real, imag], axis=0))
+        convolved = jnp.dot(inverse[...], product, preferred_element_type=F32)
+        even, odd = exchange(convolved[:half], convolved[half:])
+        result_out[2 * pair] = even
+        result_out[2 * pair + 1] = odd
+
+    @pl.loop(1, chips)
+    def _(off):
+        pair = lax.rem(chip + off, chips)
+        make_result(pair)
+        result_copy(2 * pair, 2 * off).start()
+        result_copy(2 * pair + 1, 2 * off + 1).start()
+
+    make_result(chip)
+    result_copy(sibling, 0).start()
+    own = pltpu.make_async_copy(result_out.at[me], result_in.at[me], result_got.at[me])
+    own.start()
+
+    @pl.loop(0, chips)
+    def _(step):
+        off = lax.rem(step + 1, chips)
+        tile = lax.rem(chip + chips - off, chips)
+        arrived(result_in.at[2 * tile], result_got.at[2 * tile])
+        arrived(result_in.at[2 * tile + 1], result_got.at[2 * tile + 1])
+        top, bottom = exchange(result_in[2 * tile], result_in[2 * tile + 1])
+        convolved = jnp.concatenate([top, bottom], axis=0)
+        columns = pl.ds(pl.multiple_of(tile * LANES, LANES), LANES)
+        out[:, columns] = (query[:, columns] * (convolved + direct[:, columns])).astype(BF16)
+
+    taps_pass(0).wait_send()
+    signal_copy(sibling, 0).wait_send()
+    result_copy(sibling, 0).wait_send()
+
+    @pl.loop(1, chips)
+    def _(off):
+        taps_copy(off).wait_send()
+        taps_pass(off).wait_send()
+        tile = lax.rem(chip + off, chips)
+        signal_copy(2 * tile, 2 * off).wait_send()
+        signal_copy(2 * tile + 1, 2 * off + 1).wait_send()
+        result_copy(2 * tile, 2 * off).wait_send()
+        result_copy(2 * tile + 1, 2 * off + 1).wait_send()
+
+
+def per_device_blocks(projected, short_filter, filter_taps, bank, skip):
+    steps = projected.shape[0]
+    shards = lax.axis_size("context")
+    channels = skip.shape[0]
+    half = steps // 2
+    forward, inverse = block_tables(steps)
+    packed = (shards, half, LANES)
+    spectra = (shards, 2 * steps, LANES)
+    return pl.pallas_call(
+        functools.partial(kernel, shards),
+        out_shape=jax.ShapeDtypeStruct((steps, channels), BF16),
+        in_specs=[pl.BlockSpec(memory_space=pltpu.VMEM)] * 7,
+        out_specs=pl.BlockSpec(memory_space=pltpu.VMEM),
+        scratch_shapes=[
+            pltpu.VMEM((16, 3 * channels), BF16),
+            pltpu.VMEM(packed, F32),
+            pltpu.VMEM(packed, F32),
+            pltpu.VMEM((shards, steps, LANES), BF16),
+            pltpu.VMEM((steps, channels), F32),
+            pltpu.VMEM((steps, channels), F32),
+            pltpu.VMEM(spectra, F32),
+            pltpu.VMEM(spectra, F32),
+            pltpu.VMEM(spectra, F32),
+            pltpu.VMEM(packed, F32),
+            pltpu.VMEM(packed, F32),
+            pltpu.SemaphoreType.DMA((2,)),
+            pltpu.SemaphoreType.DMA((shards,)),
+            pltpu.SemaphoreType.DMA((shards,)),
+            pltpu.SemaphoreType.DMA((shards // 2,)),
+            pltpu.SemaphoreType.DMA((shards // 2,)),
+            pltpu.SemaphoreType.DMA((shards,)),
+            pltpu.SemaphoreType.DMA((shards,)),
+            pltpu.SemaphoreType.DMA((shards,)),
+        ],
+        compiler_params=pltpu.CompilerParams(
+            collective_id=0, has_side_effects=True, vmem_limit_bytes=40 * 1024 * 1024
+        ),
+    )(
+        projected,
+        short_filter,
+        filter_taps,
+        bank.reshape(channels // LANES, LANES),
+        skip.reshape(channels // LANES, LANES),
+        jnp.asarray(forward),
+        jnp.asarray(inverse),
+    )
+
+
+def per_device(projected, short_filter, filter_taps, bank, skip):
+    shards = lax.axis_size("context")
+    half_tile = skip.shape[0] // shards == LANES // 2 and filter_taps.shape[1] == LANES // 2
+    if half_tile and shards % 2 == 0 and projected.shape[0] % 32 == 0:
+        return per_device_blocks(projected, short_filter, filter_taps, bank, skip)
+    return per_device_spectral(projected, short_filter, filter_taps, bank, skip)
+
+
 def solution(mesh):
     in_specs = (P(("groups", "context"), None), P(), P("context", None), P(), P())
     out_specs = P(("groups", "context"), None)

time: 448 us -> 42.9 us (0.10)
  the two profiles are of different devices: /device:TPU:0 before, /device:TPU:15 now
where the time goes in v1:
time: 42.9 us; the launch traced here: 42.7 us
  Pallas kernels  38 us (89%)
  local copies, waits for them, and re-layouts  4.58 us (11%)
    pallas_call x1, Pallas kernels, per_device_blocks(): pl.pallas_call(functools.partial(kernel, shards), out_shape=jax.ShapeDtyp...  38 us
    unnamed x14, local copies, waits for them, and re-layouts  4.58 us

profile of v1, /device:TPU:15, one launch (start us, length us, event | category | flops | bytes accessed | tf_op | source)
XLA Modules:
  0.0 42.7 jit_solution(594431771910675709)
XLA Ops:
  0.0 0.0 copy-start.3
  0.0 0.0 copy-start.4
  0.0 0.0 copy-start.5
  0.0 0.9 %copy.8.taps = f32[128,64]{1,0:T(8,128)S(1)} copy(f32[128,64]{0,1:T(8,128)} %param.9) | data formatting | bytes 65536 | tf_op args[2]
  0.9 0.0 copy-done.3
  0.9 0.0 copy-done.4
  0.9 0.0 copy-done.5
  0.9 0.0 copy-start
  0.9 1.1 %copy-done = bf16[128,3072]{1,0:T(8,128)(2,1)S(1)} copy-done((bf16[128,3072]{1,0:T(8,128)(2,1)S(1)}, bf16[128,3072]{1,0:T(8,128)(2,1)}, u32[]{:S(2)}) %copy-start) | copy-done | bytes 786456
  2.1 0.0 copy-start.1
  2.1 0.9 %copy-done.1 = bf16[128,768]{1,0:T(8,128)(2,1)S(1)} copy-done((bf16[128,768]{1,0:T(8,128)(2,1)S(1)}, bf16[128,768]{1,0:T(8,128)(2,1)}, u32[]{:S(2)}) %copy-start.1) | copy-done | bytes 196632
  3.0 0.0 copy-start.2
  3.0 0.9 %copy-done.2 = bf16[256,384]{1,0:T(8,128)(2,1)S(1)} copy-done((bf16[256,384]{1,0:T(8,128)(2,1)S(1)}, bf16[256,384]{1,0:T(8,128)(2,1)}, u32[]{:S(2)}) %copy-start.2) | copy-done | bytes 196632
  3.9 38.0 %shard_map.73 = bf16[128,1024]{1,0:T(8,128)(2,1)S(1)} custom-call(bf16[128,3072]{1,0:T(8,128)(2,1)S(1)} %copy-done, bf16[3,3072]{1,0:T(4,128)(2,1)S(1)} %copy-done.3, f32[128,64]{1,0:T(8,128)S(1)} %copy.8.taps, s32[8,128]{1,0:T(8,128)S(1)} %bitcast.2, f32[8,128]{1,0:T(8,128)S(1)} %bitcast.3, bf16[256,384]{1,0:T(8,128)(2,1)S(1)} %copy-done.2, ...), custom_call_target="tpu_custom_call" | custom-call | tf_op jit(solution)/shard_map/pallas_call | solution.py:478
  42.0 0.7 %copy.10 = bf16[128,1024]{1,0:T(8,128)(2,1)} copy(bf16[128,1024]{1,0:T(8,128)(2,1)S(1)} %shard_map.73) | data formatting | bytes 524288
Async XLA Ops:
  0.0 0.9 %copy-start.3 = (bf16[3,3072]{1,0:T(4,128)(2,1)S(1)}, bf16[3,3072]{1,0:T(4,128)(2,1)}, u32[]{:S(2)}) copy-start(bf16[3,3072]{1,0:T(4,128)(2,1)} %short_filter.1) | copy-start | bytes 55300
  0.0 0.9 %copy-start.4 = (s32[1024]{0:T(1024)S(1)}, s32[1024]{0:T(1024)}, u32[]{:S(2)}) copy-start(s32[1024]{0:T(1024)} %param.10) | copy-start | bytes 12292
  0.0 0.9 %copy-start.5 = (f32[1024]{0:T(1024)S(1)}, f32[1024]{0:T(1024)}, u32[]{:S(2)}) copy-start(f32[1024]{0:T(1024)} %param.11) | copy-start | bytes 12292
  0.9 1.1 %copy-start = (bf16[128,3072]{1,0:T(8,128)(2,1)S(1)}, bf16[128,3072]{1,0:T(8,128)(2,1)}, u32[]{:S(2)}) copy-start(bf16[128,3072]{1,0:T(8,128)(2,1)} %projected.1) | copy-start | bytes 2359300
  2.1 0.9 %copy-start.1 = (bf16[128,768]{1,0:T(8,128)(2,1)S(1)}, bf16[128,768]{1,0:T(8,128)(2,1)}, u32[]{:S(2)}) copy-start(bf16[128,768]{1,0:T(8,128)(2,1)} %constant.5.clone.inverse) | copy-start | bytes 589828
  3.0 0.9 %copy-start.2 = (bf16[256,384]{1,0:T(8,128)(2,1)S(1)}, bf16[256,384]{1,0:T(8,128)(2,1)}, u32[]{:S(2)}) copy-start(bf16[256,384]{1,0:T(8,128)(2,1)} %constant.4.clone.forward) | copy-start | bytes 589828

commit v2 on v1

--- a/solution.py
+++ b/solution.py
@@ -142,6 +142,9 @@
 
 LANES = 128
 F32 = jnp.float32
+LEVELS = 64.0
+TOP = 32766.0
+CODE_ROWS = 16
 BF16 = jnp.bfloat16
 
 
@@ -164,16 +167,35 @@
     return jnp.concatenate([high, low, high], axis=0)
 
 
+def coded(values):
+    peak = jnp.maximum(jnp.max(jnp.abs(values), axis=0, keepdims=True), 1e-30)
+    level = jnp.ceil(jnp.log2(peak) * LEVELS)
+    whole = jnp.round(values * (jnp.exp2(level * (-1.0 / LEVELS)) * TOP)).astype(jnp.int32)
+    level = jnp.broadcast_to(level, (CODE_ROWS, LANES)).astype(jnp.int32)
+    return jnp.concatenate([whole, level], axis=0).astype(jnp.int16)
+
+
+def decoded(words):
+    numbers = words.astype(jnp.int32).astype(F32)
+    rows = numbers.shape[0] - CODE_ROWS
+    return numbers[:rows] * (jnp.exp2(numbers[rows : rows + 1] * (1.0 / LEVELS)) * (1.0 / TOP))
+
+
 def kernel(
     shards,
-    projected,
+    projected_far,
     short_filter,
-    taps,
+    taps_far,
     bank,
     skip,
+    forward_far,
+    inverse_far,
+    out,
+    projected,
+    taps,
     forward,
     inverse,
-    out,
+    load_sem,
     halo,
     signal_out,
     signal_in,
@@ -195,6 +217,14 @@
     result_got,
 ):
     me = lax.axis_index("context")
+    load_taps = pltpu.make_async_copy(taps_far, taps, load_sem.at[0])
+    load_projected = pltpu.make_async_copy(projected_far, projected, load_sem.at[1])
+    load_forward = pltpu.make_async_copy(forward_far, forward, load_sem.at[2])
+    load_inverse = pltpu.make_async_copy(inverse_far, inverse, load_sem.at[3])
+    load_taps.start()
+    load_projected.start()
+    load_forward.start()
+    load_inverse.start()
     steps = projected.shape[0]
     half = steps // 2
     channels = out.shape[1]
@@ -234,9 +264,12 @@
             device_id={"context": lax.rem(me + off, shards)},
             device_id_type=pl.DeviceIdType.MESH,
         )
-    values = jnp.concatenate([taps[:half, :], taps[half:, :]], axis=1)
+    load_taps.wait()
+    values = jnp.transpose(taps[...])
+    values = jnp.concatenate([values[:half, :], values[half:, :]], axis=1)
     high = values.astype(BF16)
     taps_in[me] = jnp.concatenate([high, (values - high.astype(F32)).astype(BF16)], axis=0)
+    load_projected.wait()
     pl.semaphore_wait(barrier, shards - 1)
 
     behind = remote(
@@ -295,8 +328,8 @@
         columns = pl.ds(pl.multiple_of(start, LANES), LANES)
         direct[:, columns] = skip[pl.ds(tile, 1), :] * mixed
         even, odd = exchange(mixed[:half], mixed[half:])
-        signal_out[2 * tile] = even
-        signal_out[2 * tile + 1] = odd
+        signal_out[2 * tile] = coded(even)
+        signal_out[2 * tile + 1] = coded(odd)
 
     @pl.loop(1, chips)
     def _(off):
@@ -321,7 +354,7 @@
         arrived(taps_in.at[slot], taps_got.at[slot])
         taps_pass(off).start()
 
-    banks = taps.shape[1]
+    banks = taps.shape[0]
     own_bank = bank[pl.ds(chip, 1), :]
     lane = lax.broadcasted_iota(jnp.int32, (1, LANES), 1)
     in_half = (lane < LANES // 2).astype(jnp.int32)
@@ -337,6 +370,9 @@
         axis=0,
     ).astype(BF16)
 
+    load_forward.wait()
+    load_inverse.wait()
+
     def taps_block(slot):
         chosen = jnp.dot(taps_in[slot], pick, preferred_element_type=F32).astype(BF16)
         high = [chosen[:half, :LANES], chosen[:half, LANES:]]
@@ -385,7 +421,7 @@
         pairs[slot, steps:] = jnp.where(left, imag, next_imag)
 
     def signal_block(slot):
-        packed = signal_in[slot]
+        packed = decoded(signal_in[slot])
         other = turned(packed)
         return stacked(
             jnp.concatenate(
@@ -426,8 +462,8 @@
         product = stacked(jnp.concatenate([real, imag], axis=0))
         convolved = jnp.dot(inverse[...], product, preferred_element_type=F32)
         even, odd = exchange(convolved[:half], convolved[half:])
-        result_out[2 * pair] = even
-        result_out[2 * pair + 1] = odd
+        result_out[2 * pair] = coded(even)
+        result_out[2 * pair + 1] = coded(odd)
 
     @pl.loop(1, chips)
     def _(off):
@@ -447,7 +483,9 @@
         tile = lax.rem(chip + chips - off, chips)
         arrived(result_in.at[2 * tile], result_got.at[2 * tile])
         arrived(result_in.at[2 * tile + 1], result_got.at[2 * tile + 1])
-        top, bottom = exchange(result_in[2 * tile], result_in[2 * tile + 1])
+        top, bottom = exchange(
+            decoded(result_in[2 * tile]), decoded(result_in[2 * tile + 1])
+        )
         convolved = jnp.concatenate([top, bottom], axis=0)
         columns = pl.ds(pl.multiple_of(tile * LANES, LANES), LANES)
         out[:, columns] = (query[:, columns] * (convolved + direct[:, columns])).astype(BF16)
@@ -473,25 +511,32 @@
     channels = skip.shape[0]
     half = steps // 2
     forward, inverse = block_tables(steps)
-    packed = (shards, half, LANES)
+    near = pl.BlockSpec(memory_space=pltpu.VMEM)
+    far = pl.BlockSpec(memory_space=pltpu.HBM)
+    packed = (shards, half + CODE_ROWS, LANES)
     spectra = (shards, 2 * steps, LANES)
     return pl.pallas_call(
         functools.partial(kernel, shards),
         out_shape=jax.ShapeDtypeStruct((steps, channels), BF16),
-        in_specs=[pl.BlockSpec(memory_space=pltpu.VMEM)] * 7,
+        in_specs=[far, near, far, near, near, far, far],
         out_specs=pl.BlockSpec(memory_space=pltpu.VMEM),
         scratch_shapes=[
+            pltpu.VMEM(projected.shape, BF16),
+            pltpu.VMEM(filter_taps.shape[::-1], F32),
+            pltpu.VMEM(forward.shape, BF16),
+            pltpu.VMEM(inverse.shape, BF16),
+            pltpu.SemaphoreType.DMA((4,)),
             pltpu.VMEM((16, 3 * channels), BF16),
-            pltpu.VMEM(packed, F32),
-            pltpu.VMEM(packed, F32),
+            pltpu.VMEM(packed, jnp.int16),
+            pltpu.VMEM(packed, jnp.int16),
             pltpu.VMEM((shards, steps, LANES), BF16),
             pltpu.VMEM((steps, channels), F32),
             pltpu.VMEM((steps, channels), F32),
             pltpu.VMEM(spectra, F32),
             pltpu.VMEM(spectra, F32),
             pltpu.VMEM(spectra, F32),
-            pltpu.VMEM(packed, F32),
-            pltpu.VMEM(packed, F32),
+            pltpu.VMEM(packed, jnp.int16),
+            pltpu.VMEM(packed, jnp.int16),
             pltpu.SemaphoreType.DMA((2,)),
             pltpu.SemaphoreType.DMA((shards,)),
             pltpu.SemaphoreType.DMA((shards,)),
@@ -507,7 +552,7 @@
     )(
         projected,
         short_filter,
-        filter_taps,
+        filter_taps.T,
         bank.reshape(channels // LANES, LANES),
         skip.reshape(channels // LANES, LANES),
         jnp.asarray(forward),

time: 42.9 us -> 39.5 us (0.921)
  the two profiles are of different devices: /device:TPU:15 before, /device:TPU:0 now
where the time goes in v2:
time: 39.5 us; the launch traced here: 39.1 us
  Pallas kernels  32.5 us (82%)
  local copies, waits for them, and re-layouts  6.56 us (17%)
    pallas_call x1, Pallas kernels, per_device_blocks(): pl.pallas_call(functools.partial(kernel, shards), out_shape=jax.ShapeDtyp...  32.5 us
    unnamed x15, local copies, waits for them, and re-layouts  6.56 us

profile of v2, /device:TPU:0, one launch (start us, length us, event | category | flops | bytes accessed | tf_op | source)
XLA Modules:
  0.0 39.1 jit_solution(12932023869032277532)
XLA Ops:
  0.0 0.0 copy-start.5
  0.0 0.7 %copy-done.5 = s32[1024]{0:T(1024)S(1)} copy-done((s32[1024]{0:T(1024)S(1)}, s32[1024]{0:T(1024)}, u32[]{:S(2)}) %copy-start.5) | copy-done | bytes 4120
  0.7 0.0 copy-start
  0.7 1.1 %copy-done = bf16[128,3072]{1,0:T(8,128)(2,1)S(1)} copy-done((bf16[128,3072]{1,0:T(8,128)(2,1)S(1)}, bf16[128,3072]{1,0:T(8,128)(2,1)}, u32[]{:S(2)}) %copy-start) | copy-done | bytes 786456
  1.8 0.0 copy-start.1
  1.8 0.9 %copy-done.1 = bf16[128,768]{1,0:T(8,128)(2,1)S(1)} copy-done((bf16[128,768]{1,0:T(8,128)(2,1)S(1)}, bf16[128,768]{1,0:T(8,128)(2,1)}, u32[]{:S(2)}) %copy-start.1) | copy-done | bytes 196632
  2.7 0.0 copy-start.2
  2.8 0.9 %copy-done.2 = bf16[256,384]{1,0:T(8,128)(2,1)S(1)} copy-done((bf16[256,384]{1,0:T(8,128)(2,1)S(1)}, bf16[256,384]{1,0:T(8,128)(2,1)}, u32[]{:S(2)}) %copy-start.2) | copy-done | bytes 196632
  3.7 0.0 copy-start.3
  3.7 0.8 %copy-done.3 = f32[128,64]{0,1:T(8,128)S(1)} copy-done((f32[128,64]{0,1:T(8,128)S(1)}, f32[128,64]{0,1:T(8,128)}, u32[]{:S(2)}) %copy-start.3) | copy-done | bytes 32792
  4.4 0.0 copy-start.4
  4.4 0.7 %copy-done.4 = bf16[3,3072]{1,0:T(4,128)(2,1)S(1)} copy-done((bf16[3,3072]{1,0:T(4,128)(2,1)S(1)}, bf16[3,3072]{1,0:T(4,128)(2,1)}, u32[]{:S(2)}) %copy-start.4) | copy-done | bytes 18456
  5.2 0.0 copy-start.6
  5.2 0.7 %copy-done.6 = f32[1024]{0:T(1024)S(1)} copy-done((f32[1024]{0:T(1024)S(1)}, f32[1024]{0:T(1024)}, u32[]{:S(2)}) %copy-start.6) | copy-done | bytes 4120
  5.9 32.5 %shard_map.73 = bf16[128,1024]{1,0:T(8,128)(2,1)S(1)} custom-call(bf16[128,3072]{1,0:T(8,128)(2,1)S(1)} %copy-done, bf16[3,3072]{1,0:T(4,128)(2,1)S(1)} %copy-done.4, f32[64,128]{1,0:T(8,128)S(1)} %bitcast.3, s32[8,128]{1,0:T(8,128)S(1)} %bitcast.4, f32[8,128]{1,0:T(8,128)S(1)} %bitcast.5, bf16[256,384]{1,0:T(8,128)(2,1)S(1)} %copy-done.2, ...), custom_call_target="tpu_custom_call" | custom-call | tf_op jit(solution)/shard_map/pallas_call | solution.py:518
  38.4 0.7 %copy.9 = bf16[128,1024]{1,0:T(8,128)(2,1)} copy(bf16[128,1024]{1,0:T(8,128)(2,1)S(1)} %shard_map.73) | data formatting | bytes 524288
Async XLA Ops:
  0.0 0.7 %copy-start.5 = (s32[1024]{0:T(1024)S(1)}, s32[1024]{0:T(1024)}, u32[]{:S(2)}) copy-start(s32[1024]{0:T(1024)} %param.10) | copy-start | bytes 12292
  0.7 1.1 %copy-start = (bf16[128,3072]{1,0:T(8,128)(2,1)S(1)}, bf16[128,3072]{1,0:T(8,128)(2,1)}, u32[]{:S(2)}) copy-start(bf16[128,3072]{1,0:T(8,128)(2,1)} %projected_far.1) | copy-start | bytes 2359300
  1.8 0.9 %copy-start.1 = (bf16[128,768]{1,0:T(8,128)(2,1)S(1)}, bf16[128,768]{1,0:T(8,128)(2,1)}, u32[]{:S(2)}) copy-start(bf16[128,768]{1,0:T(8,128)(2,1)} %constant.5.clone.inverse_far) | copy-start | bytes 589828
  2.7 0.9 %copy-start.2 = (bf16[256,384]{1,0:T(8,128)(2,1)S(1)}, bf16[256,384]{1,0:T(8,128)(2,1)}, u32[]{:S(2)}) copy-start(bf16[256,384]{1,0:T(8,128)(2,1)} %constant.4.clone.forward_far) | copy-start | bytes 589828
  3.7 0.8 %copy-start.3 = (f32[128,64]{0,1:T(8,128)S(1)}, f32[128,64]{0,1:T(8,128)}, u32[]{:S(2)}) copy-start(f32[128,64]{0,1:T(8,128)} %param.9) | copy-start | bytes 98308
  4.4 0.7 %copy-start.4 = (bf16[3,3072]{1,0:T(4,128)(2,1)S(1)}, bf16[3,3072]{1,0:T(4,128)(2,1)}, u32[]{:S(2)}) copy-start(bf16[3,3072]{1,0:T(4,128)(2,1)} %short_filter.1) | copy-start | bytes 55300
  5.2 0.7 %copy-start.6 = (f32[1024]{0:T(1024)S(1)}, f32[1024]{0:T(1024)}, u32[]{:S(2)}) copy-start(f32[1024]{0:T(1024)} %param.11) | copy-start | bytes 12292

commit v3 on v2

--- a/solution.py
+++ b/solution.py
@@ -145,6 +145,7 @@
 LEVELS = 64.0
 TOP = 32766.0
 CODE_ROWS = 16
+VMEM_BYTES = 63 * 1024 * 1024
 BF16 = jnp.bfloat16
 
 
@@ -184,15 +185,18 @@
 def kernel(
     shards,
     projected_far,
-    short_filter,
+    short_filter_far,
     taps_far,
-    bank,
-    skip,
+    bank_far,
+    skip_far,
     forward_far,
     inverse_far,
     out,
     projected,
+    short_filter,
     taps,
+    bank,
+    skip,
     forward,
     inverse,
     load_sem,
@@ -217,14 +221,22 @@
     result_got,
 ):
     me = lax.axis_index("context")
-    load_taps = pltpu.make_async_copy(taps_far, taps, load_sem.at[0])
-    load_projected = pltpu.make_async_copy(projected_far, projected, load_sem.at[1])
-    load_forward = pltpu.make_async_copy(forward_far, forward, load_sem.at[2])
-    load_inverse = pltpu.make_async_copy(inverse_far, inverse, load_sem.at[3])
-    load_taps.start()
-    load_projected.start()
-    load_forward.start()
-    load_inverse.start()
+    far = (
+        taps_far,
+        projected_far,
+        short_filter_far,
+        skip_far,
+        bank_far,
+        forward_far,
+        inverse_far,
+    )
+    near = (taps, projected, short_filter, skip, bank, forward, inverse)
+    loads = [
+        pltpu.make_async_copy(source, target, load_sem.at[number])
+        for number, (source, target) in enumerate(zip(far, near))
+    ]
+    for load in loads:
+        load.start()
     steps = projected.shape[0]
     half = steps // 2
     channels = out.shape[1]
@@ -264,12 +276,13 @@
             device_id={"context": lax.rem(me + off, shards)},
             device_id_type=pl.DeviceIdType.MESH,
         )
-    load_taps.wait()
+    loads[0].wait()
     values = jnp.transpose(taps[...])
     values = jnp.concatenate([values[:half, :], values[half:, :]], axis=1)
     high = values.astype(BF16)
     taps_in[me] = jnp.concatenate([high, (values - high.astype(F32)).astype(BF16)], axis=0)
-    load_projected.wait()
+    for load in loads[1:4]:
+        load.wait()
     pl.semaphore_wait(barrier, shards - 1)
 
     behind = remote(
@@ -354,6 +367,8 @@
         arrived(taps_in.at[slot], taps_got.at[slot])
         taps_pass(off).start()
 
+    for load in loads[4:]:
+        load.wait()
     banks = taps.shape[0]
     own_bank = bank[pl.ds(chip, 1), :]
     lane = lax.broadcasted_iota(jnp.int32, (1, LANES), 1)
@@ -370,27 +385,31 @@
         axis=0,
     ).astype(BF16)
 
-    load_forward.wait()
-    load_inverse.wait()
-
     def taps_block(slot):
         chosen = jnp.dot(taps_in[slot], pick, preferred_element_type=F32).astype(BF16)
         high = [chosen[:half, :LANES], chosen[:half, LANES:]]
         low = [chosen[half:, :LANES], chosen[half:, LANES:]]
         return jnp.concatenate(high + low + high, axis=0)
 
-    def transform(low_slot, block, spec):
-        both = jnp.concatenate([block(low_slot), block(low_slot + 1)], axis=1)
-        both = jnp.dot(forward[...], both, preferred_element_type=F32)
-        spec[low_slot] = both[:, :LANES]
-        spec[low_slot + 1] = both[:, LANES:]
-
-    @pl.loop(0, chips)
-    def _(off):
-        source = lax.rem(chip + chips - off, chips)
-        slot = 2 * source + 1 - core
-        arrived(taps_in.at[slot], taps_got.at[slot])
-        transform(2 * source, taps_block, taps_spec)
+    def transform(slots, block, spec):
+        blocks = jnp.concatenate([block(slot) for slot in slots], axis=1)
+        blocks = jnp.dot(forward[...], blocks, preferred_element_type=F32)
+        for place, slot in enumerate(slots):
+            spec[slot] = blocks[:, place * LANES : (place + 1) * LANES]
+
+    def sources(first, count):
+        found = []
+        for off in range(first, min(first + count, chips)):
+            found.append(lax.rem(chip + chips - off, chips))
+        return found
+
+    for first in range(0, chips, 4):
+        slots = []
+        for source in sources(first, 4):
+            slot = 2 * source + 1 - core
+            arrived(taps_in.at[slot], taps_got.at[slot])
+            slots += [2 * source, 2 * source + 1]
+        transform(slots, taps_block, taps_spec)
 
     sign = lax.broadcasted_iota(jnp.int32, (steps, LANES), 0)
     sign = (1 - 2 * lax.rem(sign, 2)).astype(F32)
@@ -430,13 +449,14 @@
             )
         )
 
-    @pl.loop(0, chips)
-    def _(step):
-        off = lax.rem(step + 1, chips)
-        low_slot = 2 * lax.rem(chip + chips - off, chips)
-        arrived(signal_in.at[low_slot], signal_got.at[low_slot])
-        arrived(signal_in.at[low_slot + 1], signal_got.at[low_slot + 1])
-        transform(low_slot, signal_block, signal_spec)
+    for first in range(1, chips + 1, 2):
+        slots = []
+        for off in range(first, min(first + 2, chips + 1)):
+            source = lax.rem(chip + chips - off, chips)
+            slots += [2 * source, 2 * source + 1]
+        for slot in slots:
+            arrived(signal_in.at[slot], signal_got.at[slot])
+        transform(slots, signal_block, signal_spec)
 
     def result_copy(target, index):
         return remote(
@@ -447,9 +467,8 @@
             target,
         )
 
-    def make_result(pair):
-        def add(slot, sums):
-            real, imag = sums
+    def make_product(pair):
+        def term(slot, real, imag):
             other = 2 * pair + 1 - slot
             left_real, left_imag = signal_spec[slot, :steps], signal_spec[slot, steps:]
             right_real, right_imag = pairs[other, :steps], pairs[other, steps:]
@@ -458,21 +477,27 @@
                 imag + (left_real * right_imag + left_imag * right_real),
             )
 
-        real, imag = lax.fori_loop(0, 2 * pair + 2, add, (zero, zero))
-        product = stacked(jnp.concatenate([real, imag], axis=0))
-        convolved = jnp.dot(inverse[...], product, preferred_element_type=F32)
-        even, odd = exchange(convolved[:half], convolved[half:])
-        result_out[2 * pair] = coded(even)
-        result_out[2 * pair + 1] = coded(odd)
-
-    @pl.loop(1, chips)
-    def _(off):
-        pair = lax.rem(chip + off, chips)
-        make_result(pair)
-        result_copy(2 * pair, 2 * off).start()
-        result_copy(2 * pair + 1, 2 * off + 1).start()
-
-    make_result(chip)
+        def add(step, sums):
+            return term(2 * step + 1, *term(2 * step, *sums))
+
+        real, imag = lax.fori_loop(0, pair + 1, add, (zero, zero))
+        return stacked(jnp.concatenate([real, imag], axis=0))
+
+    for first in range(1, chips + 1, 2):
+        offs = range(first, min(first + 2, chips + 1))
+        made = [lax.rem(chip + off, chips) for off in offs]
+        products = jnp.concatenate([make_product(pair) for pair in made], axis=1)
+        convolved = jnp.dot(inverse[...], products, preferred_element_type=F32)
+        for place, pair in enumerate(made):
+            block = convolved[:, place * LANES : (place + 1) * LANES]
+            even, odd = exchange(block[:half], block[half:])
+            result_out[2 * pair] = coded(even)
+            result_out[2 * pair + 1] = coded(odd)
+        for off, pair in zip(offs, made):
+            if off < chips:
+                result_copy(2 * pair, 2 * off).start()
+                result_copy(2 * pair + 1, 2 * off + 1).start()
+
     result_copy(sibling, 0).start()
     own = pltpu.make_async_copy(result_out.at[me], result_in.at[me], result_got.at[me])
     own.start()
@@ -512,20 +537,24 @@
     half = steps // 2
     forward, inverse = block_tables(steps)
     near = pl.BlockSpec(memory_space=pltpu.VMEM)
-    far = pl.BlockSpec(memory_space=pltpu.HBM)
+    far = pl.BlockSpec(memory_space=pl.ANY)
+    tiles = (channels // LANES, LANES)
     packed = (shards, half + CODE_ROWS, LANES)
     spectra = (shards, 2 * steps, LANES)
     return pl.pallas_call(
         functools.partial(kernel, shards),
         out_shape=jax.ShapeDtypeStruct((steps, channels), BF16),
-        in_specs=[far, near, far, near, near, far, far],
+        in_specs=[far] * 7,
         out_specs=pl.BlockSpec(memory_space=pltpu.VMEM),
         scratch_shapes=[
             pltpu.VMEM(projected.shape, BF16),
+            pltpu.VMEM(short_filter.shape, BF16),
             pltpu.VMEM(filter_taps.shape[::-1], F32),
+            pltpu.VMEM(tiles, jnp.int32),
+            pltpu.VMEM(tiles, F32),
             pltpu.VMEM(forward.shape, BF16),
             pltpu.VMEM(inverse.shape, BF16),
-            pltpu.SemaphoreType.DMA((4,)),
+            pltpu.SemaphoreType.DMA((7,)),
             pltpu.VMEM((16, 3 * channels), BF16),
             pltpu.VMEM(packed, jnp.int16),
             pltpu.VMEM(packed, jnp.int16),
@@ -547,7 +576,7 @@
             pltpu.SemaphoreType.DMA((shards,)),
         ],
         compiler_params=pltpu.CompilerParams(
-            collective_id=0, has_side_effects=True, vmem_limit_bytes=40 * 1024 * 1024
+            collective_id=0, has_side_effects=True, vmem_limit_bytes=VMEM_BYTES
         ),
     )(
         projected,

time: 39.5 us -> 33.9 us (0.86)
  local copies, waits for them, and re-layouts: 6.56 us -> 1.67 us
  Pallas kernels: 32.5 us -> 31.8 us
    unnamed x15 -> x1, local copies, waits for them, and re-layouts: 6.56 us -> 1.67 us
    pallas_call x1, Pallas kernels: 32.5 us -> 31.8 us  [per_device_blocks(): pl.pallas_call(functools.partial(kernel, shards), out_shape=jax.ShapeDtyp...]
where the time goes in v3:
time: 33.9 us; the launch traced here: 33.5 us
  Pallas kernels  31.8 us (94%)
  local copies, waits for them, and re-layouts  1.67 us (5%)
    pallas_call x1, Pallas kernels, per_device_blocks(): pl.pallas_call(functools.partial(kernel, shards), out_shape=jax.ShapeDtyp...  31.8 us
    unnamed x1, local copies, waits for them, and re-layouts  1.67 us

profile of v3, /device:TPU:0, one launch (start us, length us, event | category | flops | bytes accessed | tf_op | source)
XLA Modules:
  0.0 33.5 jit_solution(4100779995092189553)
XLA Ops:
  0.0 31.8 %shard_map.73 = bf16[128,1024]{1,0:T(8,128)(2,1)} custom-call(bf16[128,3072]{1,0:T(8,128)(2,1)} %projected_far.1, bf16[3,3072]{1,0:T(4,128)(2,1)} %short_filter_far.1, f32[64,128]{1,0:T(8,128)} %bitcast.3, s32[8,128]{1,0:T(8,128)} %bitcast.4, f32[8,128]{1,0:T(8,128)} %bitcast.5, bf16[256,384]{1,0:T(8,128)(2,1)} %constant.4.clone.forward_far, ...), custom_call_target="tpu_custom_call" | custom-call | tf_op jit(solution)/shard_map/pallas_call | solution.py:544
  31.9 1.7 %copy.9 = bf16[128,1024]{1,0:T(8,128)(2,1)} copy(bf16[128,1024]{1,0:T(8,128)(2,1)} %shard_map.73) | data formatting | bytes 524288

commit v4 on v3

--- a/solution.py
+++ b/solution.py
@@ -344,7 +344,7 @@
         signal_out[2 * tile] = coded(even)
         signal_out[2 * tile + 1] = coded(odd)
 
-    @pl.loop(1, chips)
+    @pl.loop(1, chips, unroll=True)
     def _(off):
         tile = lax.rem(chip + off, chips)
         make_signal(tile)
@@ -356,7 +356,7 @@
     own = pltpu.make_async_copy(signal_out.at[me], signal_in.at[me], signal_got.at[me])
     own.start()
 
-    @pl.loop(0, chips)
+    @pl.loop(0, chips, unroll=True)
     def _(tile):
         start = tile * LANES
         query[:, pl.ds(pl.multiple_of(start, LANES), LANES)] = featured(start)
@@ -432,7 +432,7 @@
     pairs[1, :steps] = jnp.where(left, real, next_real)
     pairs[1, steps:] = jnp.where(left, imag, next_imag)
 
-    @pl.loop(2, shards)
+    @pl.loop(2, shards, unroll=True)
     def _(slot):
         real, imag = window(slot - 1, slot - 2)
         next_real, next_imag = window(slot, slot - 1)
@@ -502,7 +502,7 @@
     own = pltpu.make_async_copy(result_out.at[me], result_in.at[me], result_got.at[me])
     own.start()
 
-    @pl.loop(0, chips)
+    @pl.loop(0, chips, unroll=True)
     def _(step):
         off = lax.rem(step + 1, chips)
         tile = lax.rem(chip + chips - off, chips)

time: 33.9 us -> 33.9 us (level)
  no operation moved by 1% of the time
where the time goes in v4:
time: 33.9 us; the launch traced here: 33.5 us
  Pallas kernels  31.8 us (94%)
  local copies, waits for them, and re-layouts  1.67 us (5%)
    pallas_call x1, Pallas kernels, per_device_blocks(): pl.pallas_call(functools.partial(kernel, shards), out_shape=jax.ShapeDtyp...  31.8 us
    unnamed x1, local copies, waits for them, and re-layouts  1.67 us

profile of v4, /device:TPU:0, one launch (start us, length us, event | category | flops | bytes accessed | tf_op | source)
XLA Modules:
  0.0 33.5 jit_solution(7511977541938299072)
XLA Ops:
  0.0 31.8 %shard_map.73 = bf16[128,1024]{1,0:T(8,128)(2,1)} custom-call(bf16[128,3072]{1,0:T(8,128)(2,1)} %projected_far.1, bf16[3,3072]{1,0:T(4,128)(2,1)} %short_filter_far.1, f32[64,128]{1,0:T(8,128)} %bitcast.3, s32[8,128]{1,0:T(8,128)} %bitcast.4, f32[8,128]{1,0:T(8,128)} %bitcast.5, bf16[256,384]{1,0:T(8,128)(2,1)} %constant.4.clone.forward_far, ...), custom_call_target="tpu_custom_call" | custom-call | tf_op jit(solution)/shard_map/pallas_call | solution.py:544
  31.9 1.7 %copy.9 = bf16[128,1024]{1,0:T(8,128)(2,1)} copy(bf16[128,1024]{1,0:T(8,128)(2,1)} %shard_map.73) | data formatting | bytes 524288
